TPU v7x, 256 devices: a whole 4x4x8 slice. The times are simulated.
256 devices in a mesh: pair: 32 (over x, y, core), virt: 8 (over z).
Axes of the slice: x: 4, y: 4, z: 8, core: 2. Of those that a mesh axis runs over, the one named last changes fastest.
Arguments:
- amps: float32 [8, 2048, 2048], P(None, 'pair', 'virt'), may hold values from -6 to 6
- ints: float32 [8, 2048, 2048], P(None, 'pair', 'virt'), may hold values from -0.125 to 0.125
- panel_of: int32 [32], replicated, may hold values from 0 to 31, each once
- e_occ: float32 [8], replicated, may hold values from -2 to -0.5
- e_vir: float32 [2048], replicated, may hold values from 0.2 to 3
Outputs:
- cycle_update: float32 [8, 8, 2048, 2048], P('virt', None, 'pair')
Inputs may be any that keep to these rules, and one draw needn't show every extreme that they name: panel_of holds each of 0 to 31 once.
All inputs are finite; a program needn't handle non-finite values.
Results may differ from a plain program's by a relative error of at most 0.00007.
Values sent between devices are 32-bit elements; how exact they have to be, the bound alone decides.
No kernel may reach another device: no remote copies, remote signals or barrier semaphores. Data moves between devices by JAX's collectives and lax.ppermute only.
A program may use at most 192 MiB of HBM per device.

v0:
```python
import jax
import jax.numpy as jnp
from jax import lax
from jax.sharding import PartitionSpec as P


def panel_table(panel_of):
    count = panel_of.shape[0]
    targets = jnp.arange(count, dtype=jnp.int32)
    return (panel_of[:, None] == targets[None, :]).astype(jnp.float32)


def body(amps, ints, panel_of, e_occ, e_vir):
    panel = amps.shape[1]
    occ_all = amps.shape[0]
    n_virt = lax.axis_size("virt")
    n_pair = lax.axis_size("pair")
    occ_dev = occ_all // n_virt
    virtuals = e_vir.shape[0]
    placing = panel_table(panel_of)
    my_occ = lax.axis_index("virt") * occ_dev + jnp.arange(occ_dev, dtype=jnp.int32)
    b_rows = lax.axis_index("pair") * panel + jnp.arange(panel, dtype=jnp.int32)
    e_b = e_vir[b_rows]
    denom = (
        e_occ[my_occ][:, None, None, None]
        + e_occ[None, :, None, None]
        - e_b[None, None, :, None]
        - e_vir[None, None, None, :]
    )
    own_rows = lax.all_to_all(amps, "virt", split_axis=0, concat_axis=2, tiled=True)
    int_full = lax.all_gather(ints, "virt", axis=2, tiled=True)
    product = jnp.einsum(
        "xac,jbc->xjba",
        lax.all_gather(own_rows, "pair", axis=1, tiled=True),
        int_full,
        precision=lax.Precision.HIGHEST,
        preferred_element_type=jnp.float32,
    )
    grouped = product.reshape(occ_dev, occ_all, panel, n_pair, panel)
    direct = jnp.einsum(
        "xjbqp,qn->xjbnp",
        grouped,
        placing,
        precision=lax.Precision.HIGHEST,
        preferred_element_type=jnp.float32,
    ).reshape(occ_dev, occ_all, panel, virtuals)
    mirrored = lax.all_to_all(direct, "virt", split_axis=1, concat_axis=1, tiled=True)
    return (direct - mirrored) / denom


def solution(mesh):
    in_specs = (P(None, "pair", "virt"), P(None, "pair", "virt"), P(), P(), P())
    out_specs = P("virt", None, "pair", None)
    return jax.shard_map(body, mesh=mesh, in_specs=in_specs, out_specs=out_specs, check_vma=False)
```

profile of v0, /device:TPU:1, one launch (start us, length us, event | category | flops | bytes accessed | tf_op | source)
XLA Modules:
  0.0 342.6 jit_solution(10947563948808677150)
XLA Ops:
  6.5 0.0 all-gather.3.cloned.1.call-start
  6.5 0.7 all-gather.3.cloned.1.call-update
  7.3 0.0 all-gather.5.cloned.1.call-start
  7.3 26.2 %all_to_all.23 = f32[8,64,256]{2,1,0:T(8,128)S(1)} all-to-all(f32[8,64,256]{2,1,0:T(8,128)} %param.5), channel_id=1, replica_groups=mesh['pair'=32,'virt'=8] {'virt'}, dimensions={0} | all-to-all | bytes 1048576 | tf_op jit(solution)/shard_map/all_to_all | solution.py:30
  33.5 0.8 copy.14
  34.3 0.0 all-gather.5.cloned.1.call-update
  34.4 37.2 %all-gather.3.cloned.1.call-done = f32[8,64,2048]{2,1,0:T(8,128)} async-done(((f32[8,64,256]{2,1,0:T(8,128)}), f32[8,64,2048]{2,1,0:T(8,128)}) %all-gather.3.cloned.1.call-update) | async-done | bytes 4194320 | tf_op jit(solution)/shard_map/all_gather | solution.py:31
  71.6 79.3 %all-gather.5.cloned.1.call-done = f32[1,2048,2048]{2,1,0:T(8,128)} async-done(((f32[1,64,2048]{2,1,0:T(8,128)}), f32[1,2048,2048]{2,1,0:T(8,128)}) %all-gather.5.cloned.1.call-update) | async-done | bytes 16777232 | tf_op jit(solution)/shard_map/all_gather | solution.py:34
  150.9 0.0 copy-start.1
  150.9 57.1 %fusion.2 = f32[8,64,32,64]{3,1,2,0:T(8,128)S(1)} fusion(f32[32,64,2048,1]{2,1,0,3:T(8,128)} %bitcast.38, f32[8,64,2048]{2,1,0:T(8,128)} %all-gather.3.cloned.1.call-done), kind=kOutput, calls=%fused_computation.3 | convolution fusion | flops 25769803776 | bytes 25165824 | tf_op jit(solution)/shard_map/xac,jbc->xjba/dot_general | solution.py:32
  208.0 0.0 copy-done.1
  208.0 10.1 %fusion.4 = f32[1,8,64,32,64]{4,3,2,1,0:T(8,128)} fusion(f32[8,64,32,64]{3,1,2,0:T(8,128)S(1)} %fusion.2, s32[32]{0:T(128)S(1)} %copy-done.1), kind=kOutput, calls=%fused_computation.6 | convolution fusion | flops 402654208 | bytes 8388736 | tf_op jit(solution)/shard_map/xjbqp,qn->xjbnp/dot_general | solution.py:40
  218.1 7.8 %reshape.79 = f32[1,8,64,2048]{3,2,1,0:T(8,128)} reshape(f32[1,8,64,32,64]{4,3,2,1,0:T(8,128)} %fusion.4) | data formatting | bytes 8388608 | tf_op jit(solution)/shard_map/reshape | solution.py:46
  225.9 0.0 copy-start
  225.9 0.0 copy-start.2
  225.9 6.9 %all-to-all-start.1 = ((f32[1,8,64,2048]{3,2,0,1:T(8,128)}), f32[1,8,64,2048]{3,2,0,1:T(8,128)}, u32[]{:S(2)}, u32[]{:S(2)}) async-start(f32[1,8,64,2048]{3,2,0,1:T(8,128)} %bitcast.35), calls=%async_computation.1 | async-start | bytes 8388608 | tf_op jit(solution)/shard_map/all_to_all | solution.py:47
  232.8 0.0 copy-done
  232.8 0.8 gather_fusion
  233.6 0.0 copy-done.2
  233.6 0.6 dynamic-slice.2
  234.2 0.6 broadcast_add_fusion
  234.8 0.1 broadcast_subtract_fusion
  234.8 94.8 %all-to-all-done.1 = f32[1,8,64,2048]{3,2,0,1:T(8,128)} async-done(((f32[1,8,64,2048]{3,2,0,1:T(8,128)}), f32[1,8,64,2048]{3,2,0,1:T(8,128)}, u32[]{:S(2)}, u32[]{:S(2)}) %all-to-all-start.1) | async-done | bytes 4194336 | tf_op jit(solution)/shard_map/all_to_all | solution.py:47
  329.6 6.1 %divide_bitcast_fusion = f32[1,8,64,2048]{3,2,1,0:T(8,128)} fusion(f32[1,8,64,2048]{3,2,0,1:T(8,128)} %all-to-all-done.1, f32[2048]{0:T(1024)S(1)} %copy-done, f32[8,64]{1,0:T(8,128)S(1)} %broadcast_subtract_fusion, f32[1,8,64,2048]{3,2,1,0:T(8,128)} %reshape.79), kind=kLoop, calls=%fused_computation.5 | loop fusion | flops 3145728 | bytes 12593152 | tf_op jit(solution)/shard_map/div | solution.py:48
  (2 shorter events, 0.0 us)
Async XLA Ops:
  6.5 65.0 %all-gather.3.cloned.1.call-start = ((), (), s32[]{:S(2)}) async-start(), calls=%async_computation.2 | async-start | bytes 4718592 | tf_op jit(solution)/shard_map/all_gather | solution.py:31
  7.3 143.7 %all-gather.5.cloned.1.call-start = ((), (), s32[]{:S(2)}) async-start(), calls=%async_computation.3 | async-start | bytes 17301504 | tf_op jit(solution)/shard_map/all_gather | solution.py:34
  150.9 57.1 %copy-start.1 = (s32[32]{0:T(128)S(1)}, s32[32]{0:T(128)}, u32[]{:S(2)}) copy-start(s32[32]{0:T(128)} %param.7) | copy-start | bytes 388
  225.9 6.9 %copy-start = (f32[2048]{0:T(1024)S(1)}, f32[2048]{0:T(1024)}, u32[]{:S(2)}) copy-start(f32[2048]{0:T(1024)} %param.9) | copy-start | bytes 24580
  225.9 7.7 %copy-start.2 = (f32[8]{0:T(128)S(1)}, f32[8]{0:T(128)}, u32[]{:S(2)}) copy-start(f32[8]{0:T(128)} %param.8) | copy-start | bytes 100
  225.9 103.7 %all-to-all-start.1 = ((f32[1,8,64,2048]{3,2,0,1:T(8,128)}), f32[1,8,64,2048]{3,2,0,1:T(8,128)}, u32[]{:S(2)}, u32[]{:S(2)}) async-start(f32[1,8,64,2048]{3,2,0,1:T(8,128)} %bitcast.35), calls=%async_computation.1 | async-start | bytes 8388608 | tf_op jit(solution)/shard_map/all_to_all | solution.py:47
Sparse Core Ops, SparseCore 0:
  9.1 62.3 all-gather.2
  74.1 76.7 all-gather.4
where the time goes:
time: 343 us
  waiting for transfers between devices  212 us (62%)
  matrix products  67.2 us (20%)
  blocking collectives  26.2 us (8%)
  between operations  13.4 us (4%)
  local copies, waits for them, and re-layouts  10 us (3%)
  starting transfers between devices  6.91 us (2%)
  other arithmetic  6.76 us (2%)
    all_to_all x1, waiting for transfers between devices, body(): lax.all_to_all(direct, 'virt', split_axis=1, concat_axis=1, tiled=True)  94.8 us
    all_gather x1, waiting for transfers between devices, body(): lax.all_gather(own_rows, 'pair', axis=1, tiled=True)  79.3 us
    dot_general x1, matrix products, body(): jnp.einsum('xac,jbc->xjba', lax.all_gather(own_rows, 'pair', axis=1, tile...  57.1 us
    all_gather x1, waiting for transfers between devices, body(): int_full = lax.all_gather(ints, 'virt', axis=2, tiled=True)  37.2 us
    all_to_all x1, blocking collectives, body(): lax.all_to_all(amps, 'virt', split_axis=0, concat_axis=2, tiled=True)  26.2 us
    dot_general x1, matrix products, body(): jnp.einsum('xjbqp,qn->xjbnp', grouped, placing, precision=lax.Precision.H...  10.1 us
    reshape x1, local copies, waits for them, and re-layouts, body(): direct = jnp.einsum('xjbqp,qn->xjbnp', grouped, placing, precision=lax.Pr...  7.81 us
    all_to_all x1, starting transfers between devices, body(): lax.all_to_all(direct, 'virt', split_axis=1, concat_axis=1, tiled=True)  6.87 us
  transfers between devices with their start and end apart: 3, of which 3 were waited for; matrix products, arithmetic and copies ran while one was open for 1% of the time, Pallas kernels for 0%

commit v1 on v0

--- a/solution.py
+++ b/solution.py
@@ -31,7 +31,9 @@
     int_full = lax.all_gather(ints, "virt", axis=2, tiled=True)
     product = jnp.einsum(
         "xac,jbc->xjba",
-        lax.all_gather(own_rows, "pair", axis=1, tiled=True),
+        jnp.concatenate(
+            lax.all_to_all(jnp.stack([own_rows] * lax.axis_size("pair")), "pair", 0, 0), axis=1
+        ),
         int_full,
         precision=lax.Precision.HIGHEST,
         preferred_element_type=jnp.float32,

time: 343 us -> 506 us (1.48)
  the two profiles are of different devices: /device:TPU:1 before, /device:TPU:44 now
where the time goes in v1:
time: 506 us; the launch traced here: 505 us
  waiting for transfers between devices  362 us (72%)
  matrix products  67.2 us (13%)
  blocking collectives  24.6 us (5%)
  local copies, waits for them, and re-layouts  17.1 us (3%)
  starting transfers between devices  13.6 us (3%)
  between operations  13.5 us (3%)
  other arithmetic  6.85 us (1%)
    all_to_all x1, waiting for transfers between devices, body(): lax.all_to_all(jnp.stack([own_rows] * lax.axis_size('pair')), 'pair', 0, 0)  217 us
    all_to_all x1, waiting for transfers between devices, body(): lax.all_to_all(direct, 'virt', split_axis=1, concat_axis=1, tiled=True)  92.7 us
    dot_general x1, matrix products, body(): jnp.einsum('xac,jbc->xjba', jnp.concatenate(lax.all_to_all(jnp.stack([own...  57.1 us
    all_gather x1, waiting for transfers between devices, body(): int_full = lax.all_gather(ints, 'virt', axis=2, tiled=True)  52 us
    all_to_all x1, blocking collectives, body(): lax.all_to_all(amps, 'virt', split_axis=0, concat_axis=2, tiled=True)  24.6 us
  transfers between devices with their start and end apart: 3, of which 3 were waited for; matrix products, arithmetic and copies ran while one was open for 0% of the time, Pallas kernels for 0%

profile of v1, /device:TPU:44, one launch (start us, length us, event | category | flops | bytes accessed | tf_op | source)
XLA Modules:
  0.0 505.2 jit_solution(15914232850551647834)
XLA Ops:
  6.5 24.6 %all_to_all.25 = f32[8,64,256]{2,1,0:T(8,128)S(1)} all-to-all(f32[8,64,256]{2,1,0:T(8,128)} %param.5), channel_id=1, replica_groups=mesh['pair'=32,'virt'=8] {'virt'}, dimensions={0} | all-to-all | bytes 1048576 | tf_op jit(solution)/shard_map/all_to_all | solution.py:30
  31.2 7.9 %stack.5 = f32[32,1,64,2048]{3,2,1,0:T(8,128)} broadcast(f32[64,2048]{1,0:T(8,128)S(1)} %bitcast.39), dimensions={2,3} | broadcast | bytes 17301504 | tf_op jit(solution)/shard_map/stack | solution.py:35
  39.0 7.5 %all-to-all-start.1 = ((f32[32,1,64,2048]{3,2,1,0:T(8,128)}), f32[32,1,64,2048]{3,2,1,0:T(8,128)}, u32[]{:S(2)}, u32[]{:S(2)}) async-start(f32[32,1,64,2048]{3,2,1,0:T(8,128)} %stack.5), calls=%async_computation.1 | async-start | bytes 33554432 | tf_op jit(solution)/shard_map/all_to_all | solution.py:35
  46.6 0.0 all-gather.2.cloned.1.call-start
  46.6 0.7 all-gather.2.cloned.1.call-update
  47.3 0.0 copy-start.1
  47.3 52.0 %all-gather.2.cloned.1.call-done = f32[8,64,2048]{2,1,0:T(8,128)} async-done(((f32[8,64,256]{2,1,0:T(8,128)}), f32[8,64,2048]{2,1,0:T(8,128)}) %all-gather.2.cloned.1.call-update) | async-done | bytes 4194320 | tf_op jit(solution)/shard_map/all_gather | solution.py:31
  99.4 216.9 %all-to-all-done.1 = f32[32,1,64,2048]{3,2,1,0:T(8,128)} async-done(((f32[32,1,64,2048]{3,2,1,0:T(8,128)}), f32[32,1,64,2048]{3,2,1,0:T(8,128)}, u32[]{:S(2)}, u32[]{:S(2)}) %all-to-all-start.1) | async-done | bytes 16777248 | tf_op jit(solution)/shard_map/all_to_all | solution.py:35
  316.3 57.1 %fusion = f32[8,64,32,64]{3,1,2,0:T(8,128)S(1)} fusion(f32[32,1,64,2048]{3,2,1,0:T(8,128)} %all-to-all-done.1, f32[8,64,2048]{2,1,0:T(8,128)} %all-gather.2.cloned.1.call-done), kind=kOutput, calls=%fused_computation.1 | convolution fusion | flops 25769803776 | bytes 25165824 | tf_op jit(solution)/shard_map/xac,jbc->xjba/dot_general | solution.py:32
  373.4 0.0 copy-done.1
  373.4 10.1 %fusion.5 = f32[1,8,64,32,64]{4,3,2,1,0:T(8,128)} fusion(f32[8,64,32,64]{3,1,2,0:T(8,128)S(1)} %fusion, s32[32]{0:T(128)S(1)} %copy-done.1), kind=kOutput, calls=%fused_computation.7 | convolution fusion | flops 402654208 | bytes 8388736 | tf_op jit(solution)/shard_map/xjbqp,qn->xjbnp/dot_general | solution.py:42
  383.5 7.8 %reshape.86 = f32[1,8,64,2048]{3,2,1,0:T(8,128)} reshape(f32[1,8,64,32,64]{4,3,2,1,0:T(8,128)} %fusion.5) | data formatting | bytes 8388608 | tf_op jit(solution)/shard_map/reshape | solution.py:48
  391.3 0.0 copy-start
  391.3 0.0 copy-start.2
  391.3 6.0 %all-to-all-start.2 = ((f32[1,8,64,2048]{3,2,0,1:T(8,128)}), f32[1,8,64,2048]{3,2,0,1:T(8,128)}, u32[]{:S(2)}, u32[]{:S(2)}) async-start(f32[1,8,64,2048]{3,2,0,1:T(8,128)} %bitcast.38), calls=%async_computation.2 | async-start | bytes 8388608 | tf_op jit(solution)/shard_map/all_to_all | solution.py:49
  397.4 0.0 copy-done
  397.4 0.8 gather_fusion
  398.1 0.0 copy-done.2
  398.1 0.6 dynamic-slice.2
  398.8 0.7 broadcast_add_fusion
  399.5 0.1 broadcast_subtract_fusion
  399.5 92.7 %all-to-all-done.2 = f32[1,8,64,2048]{3,2,0,1:T(8,128)} async-done(((f32[1,8,64,2048]{3,2,0,1:T(8,128)}), f32[1,8,64,2048]{3,2,0,1:T(8,128)}, u32[]{:S(2)}, u32[]{:S(2)}) %all-to-all-start.2) | async-done | bytes 4194336 | tf_op jit(solution)/shard_map/all_to_all | solution.py:49
  492.2 6.1 %divide_bitcast_fusion = f32[1,8,64,2048]{3,2,1,0:T(8,128)} fusion(f32[1,8,64,2048]{3,2,0,1:T(8,128)} %all-to-all-done.2, f32[2048]{0:T(1024)S(1)} %copy-done, f32[8,64]{1,0:T(8,128)S(1)} %broadcast_subtract_fusion, f32[1,8,64,2048]{3,2,1,0:T(8,128)} %reshape.86), kind=kLoop, calls=%fused_computation.6 | loop fusion | flops 3145728 | bytes 12593152 | tf_op jit(solution)/shard_map/div | solution.py:50
  (3 shorter events, 0.1 us)
Async XLA Ops:
  39.0 277.3 %all-to-all-start.1 = ((f32[32,1,64,2048]{3,2,1,0:T(8,128)}), f32[32,1,64,2048]{3,2,1,0:T(8,128)}, u32[]{:S(2)}, u32[]{:S(2)}) async-start(f32[32,1,64,2048]{3,2,1,0:T(8,128)} %stack.5), calls=%async_computation.1 | async-start | bytes 33554432 | tf_op jit(solution)/shard_map/all_to_all | solution.py:35
  46.6 52.8 %all-gather.2.cloned.1.call-start = ((), (), s32[]{:S(2)}) async-start(), calls=%async_computation.3 | async-start | bytes 4718592 | tf_op jit(solution)/shard_map/all_gather | solution.py:31
  47.3 326.1 %copy-start.1 = (s32[32]{0:T(128)S(1)}, s32[32]{0:T(128)}, u32[]{:S(2)}) copy-start(s32[32]{0:T(128)} %param.7) | copy-start | bytes 388
  391.3 6.0 %copy-start = (f32[2048]{0:T(1024)S(1)}, f32[2048]{0:T(1024)}, u32[]{:S(2)}) copy-start(f32[2048]{0:T(1024)} %param.9) | copy-start | bytes 24580
  391.3 6.8 %copy-start.2 = (f32[8]{0:T(128)S(1)}, f32[8]{0:T(128)}, u32[]{:S(2)}) copy-start(f32[8]{0:T(128)} %param.8) | copy-start | bytes 100
  391.3 100.9 %all-to-all-start.2 = ((f32[1,8,64,2048]{3,2,0,1:T(8,128)}), f32[1,8,64,2048]{3,2,0,1:T(8,128)}, u32[]{:S(2)}, u32[]{:S(2)}) async-start(f32[1,8,64,2048]{3,2,0,1:T(8,128)} %bitcast.38), calls=%async_computation.2 | async-start | bytes 8388608 | tf_op jit(solution)/shard_map/all_to_all | solution.py:49
Sparse Core Ops, SparseCore 0:
  49.2 50.1 all-gather.1
